TPU v7x, 32 devices: a whole 2x2x4 slice. The times are simulated.
32 devices in a mesh: parts: 2 (over y), track: 4 (over z), tm: 2 (over x), coef: 2 (over core).
Axes of the slice: x: 2, y: 2, z: 4, core: 2. Of those that a mesh axis runs over, the one named last changes fastest.
Arguments:
- sector_ids: int32 [12288], P(('parts', 'track', 'tm')), parts along dimension 0, may hold values from 0 to 63, as said below
- observed: float32 [3, 12288], P(None, ('parts', 'track', 'tm')), parts along dimension 1, may hold values from -6 to 6
- weights: float32 [3, 12288], P(None, ('parts', 'track', 'tm')), parts along dimension 1, may hold values from 0.3 to 3
- coefficients: float32 [2048, 128], P(('parts', 'track')), parts along dimension 0, may hold values from -6 to 6
- tile_index: int32 [128, 12], P(('parts', 'track', 'tm'), 'coef'), parts along dimension 0, may hold values from 0 to 1023, as said below
- tile_count: int32 [128], P(('parts', 'track', 'tm')), parts along dimension 0, may hold values from 3 to 12
- sensitivity: bfloat16 [128, 12, 3, 128, 128], P(('parts', 'track', 'tm'), 'coef'), parts along dimension 0, may hold values from -0.15625 to 0.15625
Outputs:
- gradient: float32 [2048, 128], P(('parts', 'track')), parts along dimension 0
There are 2 independent parts, one for each index of `parts`. A program takes and returns all parts, laid end to end along the dimension named above; each array names one. Nothing has to cross between parts.
Inputs may be any that keep to these rules, and one draw needn't show every extreme that they name: `sector_ids`: the rows of one index of track and tm fall in at most 192 rows into the 8 consecutive sectors of any one index, and some pair reaches 192; the sectors of each index receive exactly 768 rows in all; each sector holds at most 128 rows, and every index holds a sector with exactly 128. `tile_index`: entries at positions from tile_count on are arbitrary blocks and take no part. Block n belongs to track index n // 256. Of the 48 entries held by one index of track, tm and coef (its sectors' rows, its coef share of the columns), live or not, at most 24 name blocks of any one track index, and every such device has a track index named exactly 24 times.
All inputs are finite; a program needn't handle non-finite values.
Results may differ from a plain program's by a relative error of at most 0.0037.
Values may be sent and summed in bfloat16 or wider, within the bound.
A program may use at most 64 MiB of HBM per device.

v0:
```python
import jax
import jax.numpy as jnp
from jax import lax
from jax.sharding import PartitionSpec as P

HUBER = 2.0


def per_device(sector_ids, observed, weights, coefficients, tile_index, tile_count, sensitivity):
    sector_total = tile_index.shape[0]
    half_k = tile_index.shape[1]
    slot_count = sensitivity.shape[3]
    block_width = sensitivity.shape[4]
    owners = lax.axis_size(("track", "tm"))
    row_total = sector_ids.shape[0]
    capacity = 2 * row_total // owners
    rounded = coefficients.astype(jnp.bfloat16)
    every_block = lax.all_gather(rounded, "track", axis=0, tiled=True)
    owner_of = sector_ids // sector_total
    local_sector = sector_ids % sector_total
    onehot = (owner_of[:, None] == jnp.arange(owners, dtype=jnp.int32)[None, :]).astype(jnp.int32)
    ranking = jnp.sum((jnp.cumsum(onehot, axis=0) - 1) * onehot, axis=1)
    placing = owner_of * capacity + ranking
    payload = jnp.concatenate([observed, weights], axis=0)
    outgoing = jnp.zeros((6, owners * capacity), jnp.float32).at[:, placing].set(payload)
    outgoing = jnp.transpose(outgoing.reshape(6, owners, capacity), (1, 0, 2))
    labels = jnp.full((owners * capacity,), -1, jnp.int32).at[placing].set(local_sector)
    labels = labels.reshape(owners, capacity)
    got_rows, got_labels = (
        lax.all_to_all(outgoing, ("track", "tm"), split_axis=0, concat_axis=0, tiled=True),
        lax.all_to_all(labels, ("track", "tm"), split_axis=0, concat_axis=0, tiled=True),
    )
    received = jnp.transpose(got_rows, (1, 0, 2)).reshape(6, owners * capacity)
    flat_labels = got_labels.reshape(owners * capacity)
    member = (flat_labels[:, None] == jnp.arange(sector_total, dtype=jnp.int32)[None, :]).astype(
        jnp.int32
    )
    within = jnp.sum((jnp.cumsum(member, axis=0) - 1) * member, axis=1)
    target = jnp.where(
        flat_labels >= 0, flat_labels * slot_count + within, sector_total * slot_count
    )
    gridded = jnp.zeros((6, sector_total * slot_count + 1), jnp.float32).at[:, target].set(received)
    gridded = jnp.transpose(gridded[:, :-1].reshape(6, sector_total, slot_count), (1, 0, 2))
    observed_tiles = gridded[:, :3]
    weight_tiles = gridded[:, 3:]
    k_global = lax.axis_index("coef") * half_k + jnp.arange(half_k, dtype=jnp.int32)
    active = k_global[None, :] < tile_count[:, None]
    blocks = jnp.take(every_block, tile_index, axis=0)
    blocks = jnp.where(active[:, :, None], blocks, jnp.zeros_like(blocks))
    partial_pred = jnp.einsum(
        "skcjb,skb->scj", sensitivity, blocks, preferred_element_type=jnp.float32
    )
    predicted = lax.psum(partial_pred, "coef")
    scaled = weight_tiles * (predicted - observed_tiles)
    force = (weight_tiles * scaled / jnp.sqrt(1.0 + (scaled / HUBER) ** 2)).astype(jnp.bfloat16)
    tile_grad = jnp.einsum("skcjb,scj->skb", sensitivity, force, preferred_element_type=jnp.float32)
    tile_grad = jnp.where(active[:, :, None], tile_grad, jnp.zeros_like(tile_grad))
    block_total = every_block.shape[0]
    partial_grad = jnp.zeros((block_total, block_width), jnp.float32)
    partial_grad = partial_grad.at[tile_index.reshape(-1)].add(tile_grad.reshape(-1, block_width))
    summed = lax.psum_scatter(partial_grad, "track", scatter_dimension=0, tiled=True)
    gradient = lax.psum(summed, ("tm", "coef"))
    return gradient


def solution(mesh):
    placed = (
        P(("parts", "track", "tm")),
        P(None, ("parts", "track", "tm")),
        P(None, ("parts", "track", "tm")),
        P(("parts", "track"), None),
        P(("parts", "track", "tm"), "coef"),
        P(("parts", "track", "tm")),
        P(("parts", "track", "tm"), "coef", None, None, None),
    )
    return jax.shard_map(
        per_device,
        mesh=mesh,
        in_specs=placed,
        out_specs=P(("parts", "track"), None),
        check_vma=False,
    )
```

profile of v0, /device:TPU:0, one launch (start us, length us, event | category | flops | bytes accessed | tf_op | source)
XLA Modules:
  0.0 135.0 jit_solution(9949122944024813271)
XLA Ops:
  6.5 0.7 add_select_fusion
  7.2 1.7 %reduce-window.14 = s32[8,6,128]{2,0,1:T(8,128)S(1)} reduce-window(s32[8,6,128]{2,0,1:T(8,128)S(1)} %fusion.13, s32[]{:T(128)} %constant.40.clone.1), window={size=1x1x128 pad=0_0x0_0x127_0}, to_apply=%region_0.1 | reduce-window | flops 780288 | bytes 49156 | tf_op jit(solution)/shard_map/reduce-window
  8.9 0.1 slice.30
  9.0 0.1 copy.24
  9.2 0.2 reduce-window.15
  9.3 0.1 copy.25
  9.4 0.1 fusion.11
  9.5 3.4 %scatter_custom_fusion = s32[1536]{0:T(1024)S(1)} fusion(s32[768]{0:T(1024)S(1)} %compare_select_fusion.2, s32[768]{0:T(1024)S(1)} %get-tuple-element.7, s32[]{:T(128)} %constant.74.clone.1), kind=kCustom, calls=%fused_computation.50 | custom fusion | bytes 6148 | tf_op jit(solution)/shard_map/scatter | solution.py:27
  12.9 0.7 all_to_all.9
  13.6 7.3 %all-to-all-start = ((s32[8,1,192]{2,1,0:T(1,128)}), s32[8,1,192]{2,1,0:T(1,128)S(1)}, u32[]{:S(2)}, u32[]{:S(2)}) async-start(s32[8,1,192]{2,1,0:T(1,128)} %all_to_all.9), calls=%async_computation | async-start | bytes 16384 | tf_op jit(solution)/shard_map/all_to_all | solution.py:31
  20.8 0.7 compare_select_fusion.1
  21.5 0.8 reshape.166
  22.3 0.7 maximum_bitcast_fusion
  23.0 0.2 copy.26
  23.2 4.4 %scatter_custom_fusion.1 = f32[6,1536]{0,1:T(8,128)S(1)} fusion(s32[768]{0:T(1024)S(1)} %compare_select_fusion.2, f32[768,6]{1,0:T(8,128)S(1)} %copy.26, f32[]{:T(128)} %constant.39.clone.1), kind=kCustom, calls=%fused_computation.7 | custom fusion | bytes 36868 | tf_op jit(solution)/shard_map/scatter | solution.py:25
  27.6 1.0 copy.27
  28.6 0.9 convert_element_type.18
  29.5 14.5 %all_gather.3 = bf16[1024,128]{1,0:T(8,128)(2,1)S(1)} all-gather(bf16[256,128]{1,0:T(8,128)(2,1)S(1)} %convert_element_type.18), channel_id=1, replica_groups=mesh['parts'=2,'track'=4,'tm'=2,'coef'=2] {'track'}, dimensions={0}, use_global_device_ids=true | all-gather | bytes 327680 | tf_op jit(solution)/shard_map/all_gather | solution.py:18
  44.0 0.1 reshape.175
  44.0 0.6 gather_fusion
  44.7 0.8 compare_and_fusion
  45.4 0.1 select_bitcast_fusion
  45.5 3.7 %fusion = f32[8,1,3,128,1]{3,1,4,2,0:T(1,128)S(1)} fusion(bf16[8,6,3,128,128]{4,3,2,1,0:T(8,128)(2,1)} %param.13, bf16[8,6,128,1,1]{2,1,0,3,4:T(8,128)(2,1)S(1)} %select_bitcast_fusion), kind=kOutput, calls=%fused_computation.5 | convolution fusion | flops 4718592 | bytes 4743168 | tf_op jit(solution)/shard_map/skcjb,skb->scj/dot_general | solution.py:50
  49.2 3.3 %psum.14 = f32[8,3,128]{2,0,1:T(8,128)S(1)} all-reduce(f32[8,3,128]{2,0,1:T(8,128)S(1)} %bitcast.50), channel_id=1, replica_groups=mesh['parts'=2,'track'=4,'tm'=2,'coef'=2] {'coef'}, use_global_device_ids=true, to_apply=%region_9.10 | all-reduce | flops 3072 | bytes 24576 | tf_op jit(solution)/shard_map/psum | solution.py:53
  52.5 0.0 all-to-all-done
  52.5 5.7 %all-to-all-start.1 = ((f32[8,6,192]{2,1,0:T(8,128)}), f32[8,6,192]{2,1,0:T(8,128)S(1)}, u32[]{:S(2)}, u32[]{:S(2)}) async-start(f32[8,6,192]{2,1,0:T(8,128)} %bitcast.8), calls=%async_computation.1 | async-start | bytes 131072 | tf_op jit(solution)/shard_map/all_to_all | solution.py:30
  58.2 0.0 reduce-scatter.2.cloned.1.call-start
  58.3 0.1 eq.61
  58.4 0.1 eq.57
  58.5 2.3 %reduce-window.16 = s32[8,12,128]{2,1,0:T(8,128)S(1)} reduce-window(s32[8,12,128]{2,1,0:T(8,128)S(1)} %fusion.8, s32[]{:T(128)} %constant.40.clone.1), window={size=1x1x128 pad=0_0x0_0x127_0}, to_apply=%region_4.5 | reduce-window | flops 1560576 | bytes 98308 | tf_op jit(solution)/shard_map/reduce-window.2
  60.7 0.3 slice_reduce_fusion
  61.0 0.2 reduce-window.19
  61.2 0.1 add_bitcast_fusion
  61.3 0.1 mul.43
  61.4 0.1 ge.21
  61.6 3.5 %all-to-all-done.1 = f32[8,6,192]{2,1,0:T(8,128)S(1)} async-done(((f32[8,6,192]{2,1,0:T(8,128)}), f32[8,6,192]{2,1,0:T(8,128)S(1)}, u32[]{:S(2)}, u32[]{:S(2)}) %all-to-all-start.1) | async-done | bytes 36896 | tf_op jit(solution)/shard_map/all_to_all | solution.py:30
  65.1 0.1 reshape.198
  65.2 0.3 copy.29
  65.5 4.4 %scatter_custom_fusion.2 = f32[6,1025]{0,1:T(8,128)S(1)} fusion(s32[1536]{0:T(1024)S(1)} %fusion.17, f32[1536,6]{1,0:T(8,128)S(1)} %copy.29, f32[]{:T(128)} %constant.39.clone.1), kind=kCustom, calls=%fused_computation.9 | custom fusion | bytes 24604 | tf_op jit(solution)/shard_map/scatter | solution.py:42
  70.0 0.2 copy.36
  70.2 3.1 %fusion.15 = f32[8,1,6,128,1]{3,1,4,2,0:T(1,128)S(1)} fusion(bf16[8,6,3,128,128]{4,3,2,1,0:T(8,128)(2,1)} %param.13, bf16[8,3,128,1,1]{2,0,1,3,4:T(8,128)(2,1)S(1)} %fusion.18), kind=kOutput, calls=%fused_computation.34 | convolution fusion | flops 4718592 | bytes 4749312 | tf_op jit(solution)/shard_map/skcjb,scj->skb/dot_general | solution.py:56
  73.3 0.1 bitcast_select_fusion
  73.4 1.5 %scatter_custom_fusion.3 = f32[1024,128]{1,0:T(8,128)} fusion(s32[48]{0:T(128)S(1)} %fusion.23, f32[48,128]{1,0:T(8,128)S(1)} %reshape.209, f32[]{:T(128)} %constant.39.clone.1), kind=kCustom, calls=%fused_computation.11 | custom fusion | flops 6144 | bytes 524292 | tf_op jit(solution)/shard_map/scatter-add | solution.py:60
  74.9 0.0 reduce-scatter.2.cloned.1.call-update
  75.0 0.0 all-reduce.2.cloned.1.call-start
  75.0 19.6 %reduce-scatter.2.cloned.1.call-done = f32[256,128]{1,0:T(8,128)} async-done(((f32[1024,128]{1,0:T(8,128)}), f32[256,128]{1,0:T(8,128)}) %reduce-scatter.2.cloned.1.call-update) | async-done | bytes 131088 | tf_op jit(solution)/shard_map/reduce_scatter | solution.py:61
  94.6 0.0 all-reduce.2.cloned.1.call-update
  94.7 32.0 %all-reduce.2.cloned.1.call-done = f32[256,128]{1,0:T(8,128)} async-done(((f32[256,128]{1,0:T(8,128)}), f32[256,128]{1,0:T(8,128)}) %all-reduce.2.cloned.1.call-update) | async-done | bytes 131088 | tf_op jit(solution)/shard_map/psum | solution.py:62
  126.6 1.6 %copy.49 = f32[256,128]{1,0:T(8,128)} copy(f32[256,128]{1,0:T(8,128)} %all-reduce.2.cloned.1.call-done) | data formatting | bytes 262144
  (16 shorter events, 0.3 us)
Async XLA Ops:
  13.6 38.9 %all-to-all-start = ((s32[8,1,192]{2,1,0:T(1,128)}), s32[8,1,192]{2,1,0:T(1,128)S(1)}, u32[]{:S(2)}, u32[]{:S(2)}) async-start(s32[8,1,192]{2,1,0:T(1,128)} %all_to_all.9), calls=%async_computation | async-start | bytes 16384 | tf_op jit(solution)/shard_map/all_to_all | solution.py:31
  52.5 12.6 %all-to-all-start.1 = ((f32[8,6,192]{2,1,0:T(8,128)}), f32[8,6,192]{2,1,0:T(8,128)S(1)}, u32[]{:S(2)}, u32[]{:S(2)}) async-start(f32[8,6,192]{2,1,0:T(8,128)} %bitcast.8), calls=%async_computation.1 | async-start | bytes 131072 | tf_op jit(solution)/shard_map/all_to_all | solution.py:30
  58.2 36.4 %reduce-scatter.2.cloned.1.call-start = ((), (), s32[]{:S(2)}) async-start(), calls=%async_computation.3 | async-start | bytes 655360 | tf_op jit(solution)/shard_map/reduce_scatter | solution.py:61
  75.0 51.7 %all-reduce.2.cloned.1.call-start = ((), (), s32[]{:S(2)}) async-start(), calls=%async_computation.4 | async-start | bytes 262144 | tf_op jit(solution)/shard_map/psum | solution.py:62
Sparse Core Ops, SparseCore 0:
  75.1 19.5 reduce-scatter.1
  97.0 29.6 all-reduce.1
where the time goes:
time: 136 us; the launch traced here: 135 us
  waiting for transfers between devices  55.2 us (41%)
  local copies, waits for them, and re-layouts  18.6 us (14%)
  blocking collectives  17.8 us (13%)
  between operations  13.5 us (10%)
  starting transfers between devices  13.1 us (10%)
  other arithmetic  10.2 us (7%)
  matrix products  6.73 us (5%)
    psum x1, waiting for transfers between devices, per_device(): gradient = lax.psum(summed, ('tm', 'coef'))  32 us
    reduce_scatter x1, waiting for transfers between devices, per_device(): lax.psum_scatter(partial_grad, 'track', scatter_dimension=0, tiled=True)  19.6 us
    all_gather x1, blocking collectives, per_device(): every_block = lax.all_gather(rounded, 'track', axis=0, tiled=True)  14.5 us
    all_to_all x1, starting transfers between devices, per_device(): lax.all_to_all(labels, ('track', 'tm'), split_axis=0, concat_axis=0, tile...  7.25 us
    all_to_all x1, starting transfers between devices, per_device(): lax.all_to_all(outgoing, ('track', 'tm'), split_axis=0, concat_axis=0, ti...  5.72 us
    scatter x1, local copies, waits for them, and re-layouts, per_device(): jnp.zeros((6, sector_total * slot_count + 1), jnp.float32).at[:, target]  4.45 us
    scatter x1, local copies, waits for them, and re-layouts, per_device(): jnp.zeros((6, owners * capacity), jnp.float32).at[:, placing].set(payload)  4.36 us
    another operation x4, other arithmetic  4.31 us
  transfers between devices with their start and end apart: 4, of which 3 were waited for; matrix products, arithmetic and copies ran while one was open for 13% of the time, Pallas kernels for 0%

commit v1 on v0

--- a/solution.py
+++ b/solution.py
@@ -59,7 +59,7 @@
     partial_grad = jnp.zeros((block_total, block_width), jnp.float32)
     partial_grad = partial_grad.at[tile_index.reshape(-1)].add(tile_grad.reshape(-1, block_width))
     summed = lax.psum_scatter(partial_grad, "track", scatter_dimension=0, tiled=True)
-    gradient = lax.psum(summed, ("tm", "coef"))
+    gradient = jnp.sum(lax.all_gather(summed, ("tm", "coef")), axis=0)
     return gradient
 
 

time: 136 us -> 110 us (0.81)
  waiting for transfers between devices: 55.2 us -> 23.2 us
  blocking collectives: 17.8 us -> 25.1 us
  local copies, waits for them, and re-layouts: 18.6 us -> 17 us
    psum x1 -> x0, waiting for transfers between devices: 32 us -> none  [per_device(): gradient = lax.psum(summed, ('tm', 'coef'))]
    all_gather x0 -> x1, blocking collectives: none -> 7.33 us  [per_device(): gradient = jnp.sum(lax.all_gather(summed, ('tm', 'coef')), axis=0)]
    unnamed x1 -> x0, local copies, waits for them, and re-layouts: 1.57 us -> none
  transfers between devices with their start and end apart: 4 -> 3, of which waited for: 3 -> 2; matrix products, arithmetic and copies ran while one was open for 13% -> 16% of each run, Pallas kernels for 0% -> 0%
where the time goes in v1:
time: 110 us; the launch traced here: 109 us
  blocking collectives  25.1 us (23%)
  waiting for transfers between devices  23.2 us (21%)
  local copies, waits for them, and re-layouts  17 us (15%)
  between operations  13.5 us (12%)
  starting transfers between devices  13 us (12%)
  other arithmetic  10.9 us (10%)
  matrix products  6.73 us (6%)
    reduce_scatter x1, waiting for transfers between devices, per_device(): lax.psum_scatter(partial_grad, 'track', scatter_dimension=0, tiled=True)  19.7 us
    all_gather x1, blocking collectives, per_device(): every_block = lax.all_gather(rounded, 'track', axis=0, tiled=True)  14.5 us
    all_gather x1, blocking collectives, per_device(): gradient = jnp.sum(lax.all_gather(summed, ('tm', 'coef')), axis=0)  7.33 us
    all_to_all x1, starting transfers between devices, per_device(): lax.all_to_all(labels, ('track', 'tm'), split_axis=0, concat_axis=0, tile...  7.25 us
    all_to_all x1, starting transfers between devices, per_device(): lax.all_to_all(outgoing, ('track', 'tm'), split_axis=0, concat_axis=0, ti...  5.72 us
    scatter x1, local copies, waits for them, and re-layouts, per_device(): jnp.zeros((6, sector_total * slot_count + 1), jnp.float32).at[:, target]  4.45 us
    scatter x1, local copies, waits for them, and re-layouts, per_device(): jnp.zeros((6, owners * capacity), jnp.float32).at[:, placing].set(payload)  4.36 us
    another operation x4, other arithmetic  4.31 us
  transfers between devices with their start and end apart: 3, of which 2 were waited for; matrix products, arithmetic and copies ran while one was open for 16% of the time, Pallas kernels for 0%

profile of v1, /device:TPU:0, one launch (start us, length us, event | category | flops | bytes accessed | tf_op | source)
XLA Modules:
  0.0 109.5 jit_solution(10149785270307628693)
XLA Ops:
  6.5 0.7 add_select_fusion
  7.2 1.7 %reduce-window.14 = s32[8,6,128]{2,0,1:T(8,128)S(1)} reduce-window(s32[8,6,128]{2,0,1:T(8,128)S(1)} %fusion.13, s32[]{:T(128)} %constant.40.clone.1), window={size=1x1x128 pad=0_0x0_0x127_0}, to_apply=%region_0.1 | reduce-window | flops 780288 | bytes 49156 | tf_op jit(solution)/shard_map/reduce-window
  8.9 0.1 slice.30
  9.0 0.1 copy.30
  9.2 0.2 reduce-window.15
  9.3 0.1 copy.31
  9.4 0.1 fusion.11
  9.5 3.4 %scatter_custom_fusion = s32[1536]{0:T(1024)S(1)} fusion(s32[768]{0:T(1024)S(1)} %compare_select_fusion.2, s32[768]{0:T(1024)S(1)} %get-tuple-element.7, s32[]{:T(128)} %constant.44.clone.1), kind=kCustom, calls=%fused_computation.50 | custom fusion | bytes 6148 | tf_op jit(solution)/shard_map/scatter | solution.py:27
  12.9 0.7 all_to_all.9
  13.6 7.3 %all-to-all-start = ((s32[8,1,192]{2,1,0:T(1,128)}), s32[8,1,192]{2,1,0:T(1,128)S(1)}, u32[]{:S(2)}, u32[]{:S(2)}) async-start(s32[8,1,192]{2,1,0:T(1,128)} %all_to_all.9), calls=%async_computation | async-start | bytes 16384 | tf_op jit(solution)/shard_map/all_to_all | solution.py:31
  20.8 0.7 compare_select_fusion.1
  21.5 0.8 reshape.166
  22.3 0.7 maximum_bitcast_fusion
  23.0 0.2 copy.32
  23.2 4.4 %scatter_custom_fusion.1 = f32[6,1536]{0,1:T(8,128)S(1)} fusion(s32[768]{0:T(1024)S(1)} %compare_select_fusion.2, f32[768,6]{1,0:T(8,128)S(1)} %copy.32, f32[]{:T(128)} %constant.39.clone.1), kind=kCustom, calls=%fused_computation.7 | custom fusion | bytes 36868 | tf_op jit(solution)/shard_map/scatter | solution.py:25
  27.6 1.0 copy.33
  28.6 0.9 convert_element_type.18
  29.5 14.5 %all_gather.9 = bf16[1024,128]{1,0:T(8,128)(2,1)S(1)} all-gather(bf16[256,128]{1,0:T(8,128)(2,1)S(1)} %convert_element_type.18), channel_id=1, replica_groups=mesh['parts'=2,'track'=4,'tm'=2,'coef'=2] {'track'}, dimensions={0}, use_global_device_ids=true | all-gather | bytes 327680 | tf_op jit(solution)/shard_map/all_gather | solution.py:18
  44.0 0.1 reshape.175
  44.0 0.6 gather_fusion
  44.7 0.8 compare_and_fusion
  45.4 0.1 select_bitcast_fusion
  45.5 3.7 %fusion = f32[8,1,3,128,1]{3,1,4,2,0:T(1,128)S(1)} fusion(bf16[8,6,3,128,128]{4,3,2,1,0:T(8,128)(2,1)} %param.13, bf16[8,6,128,1,1]{2,1,0,3,4:T(8,128)(2,1)S(1)} %select_bitcast_fusion), kind=kOutput, calls=%fused_computation.5 | convolution fusion | flops 4718592 | bytes 4743168 | tf_op jit(solution)/shard_map/skcjb,skb->scj/dot_general | solution.py:50
  49.2 3.3 %psum.7 = f32[8,3,128]{2,0,1:T(8,128)S(1)} all-reduce(f32[8,3,128]{2,0,1:T(8,128)S(1)} %bitcast.52), channel_id=1, replica_groups=mesh['parts'=2,'track'=4,'tm'=2,'coef'=2] {'coef'}, use_global_device_ids=true, to_apply=%region_9.10 | all-reduce | flops 3072 | bytes 24576 | tf_op jit(solution)/shard_map/psum | solution.py:53
  52.5 0.0 all-to-all-done
  52.5 5.7 %all-to-all-start.1 = ((f32[8,6,192]{2,1,0:T(8,128)}), f32[8,6,192]{2,1,0:T(8,128)S(1)}, u32[]{:S(2)}, u32[]{:S(2)}) async-start(f32[8,6,192]{2,1,0:T(8,128)} %bitcast.8), calls=%async_computation.1 | async-start | bytes 131072 | tf_op jit(solution)/shard_map/all_to_all | solution.py:30
  58.2 0.0 reduce-scatter.2.cloned.1.call-start
  58.3 0.1 eq.61
  58.4 0.1 eq.57
  58.5 2.3 %reduce-window.16 = s32[8,12,128]{2,1,0:T(8,128)S(1)} reduce-window(s32[8,12,128]{2,1,0:T(8,128)S(1)} %fusion.8, s32[]{:T(128)} %constant.40.clone.1), window={size=1x1x128 pad=0_0x0_0x127_0}, to_apply=%region_4.5 | reduce-window | flops 1560576 | bytes 98308 | tf_op jit(solution)/shard_map/reduce-window.2
  60.7 0.3 slice_reduce_fusion
  61.0 0.2 reduce-window.19
  61.2 0.1 add_bitcast_fusion
  61.3 0.1 mul.43
  61.4 0.1 ge.21
  61.6 3.5 %all-to-all-done.1 = f32[8,6,192]{2,1,0:T(8,128)S(1)} async-done(((f32[8,6,192]{2,1,0:T(8,128)}), f32[8,6,192]{2,1,0:T(8,128)S(1)}, u32[]{:S(2)}, u32[]{:S(2)}) %all-to-all-start.1) | async-done | bytes 36896 | tf_op jit(solution)/shard_map/all_to_all | solution.py:30
  65.1 0.1 reshape.198
  65.2 0.3 copy.35
  65.5 4.4 %scatter_custom_fusion.2 = f32[6,1025]{0,1:T(8,128)S(1)} fusion(s32[1536]{0:T(1024)S(1)} %fusion.17, f32[1536,6]{1,0:T(8,128)S(1)} %copy.35, f32[]{:T(128)} %constant.39.clone.1), kind=kCustom, calls=%fused_computation.9 | custom fusion | bytes 24604 | tf_op jit(solution)/shard_map/scatter | solution.py:42
  70.0 0.2 copy.42
  70.2 3.1 %fusion.15 = f32[8,1,6,128,1]{3,1,4,2,0:T(1,128)S(1)} fusion(bf16[8,6,3,128,128]{4,3,2,1,0:T(8,128)(2,1)} %param.13, bf16[8,3,128,1,1]{2,0,1,3,4:T(8,128)(2,1)S(1)} %fusion.18), kind=kOutput, calls=%fused_computation.34 | convolution fusion | flops 4718592 | bytes 4749312 | tf_op jit(solution)/shard_map/skcjb,scj->skb/dot_general | solution.py:56
  73.3 0.1 bitcast_select_fusion
  73.4 1.5 %scatter_custom_fusion.3 = f32[1024,128]{1,0:T(8,128)} fusion(s32[48]{0:T(128)S(1)} %fusion.23, f32[48,128]{1,0:T(8,128)S(1)} %reshape.209, f32[]{:T(128)} %constant.39.clone.1), kind=kCustom, calls=%fused_computation.11 | custom fusion | flops 6144 | bytes 524292 | tf_op jit(solution)/shard_map/scatter-add | solution.py:60
  74.9 0.0 reduce-scatter.2.cloned.1.call-update
  75.0 19.7 %reduce-scatter.2.cloned.1.call-done = f32[256,128]{1,0:T(8,128)} async-done(((f32[1024,128]{1,0:T(8,128)}), f32[256,128]{1,0:T(8,128)}) %reduce-scatter.2.cloned.1.call-update) | async-done | bytes 131088 | tf_op jit(solution)/shard_map/reduce_scatter | solution.py:61
  94.6 7.3 %all-gather = f32[1024,128]{1,0:T(8,128)S(1)} all-gather(f32[256,128]{1,0:T(8,128)} %reduce-scatter.2.cloned.1.call-done), channel_id=2, replica_groups=mesh['parts'=2,'track'=4,'tm'=2,'coef'=2] {'tm','coef'}, dimensions={0}, use_global_device_ids=true | all-gather | bytes 655360 | tf_op jit(solution)/shard_map/all_gather | solution.py:62
  102.0 0.7 reduce_sum.32
  (16 shorter events, 0.3 us)
Async XLA Ops:
  13.6 38.9 %all-to-all-start = ((s32[8,1,192]{2,1,0:T(1,128)}), s32[8,1,192]{2,1,0:T(1,128)S(1)}, u32[]{:S(2)}, u32[]{:S(2)}) async-start(s32[8,1,192]{2,1,0:T(1,128)} %all_to_all.9), calls=%async_computation | async-start | bytes 16384 | tf_op jit(solution)/shard_map/all_to_all | solution.py:31
  52.5 12.6 %all-to-all-start.1 = ((f32[8,6,192]{2,1,0:T(8,128)}), f32[8,6,192]{2,1,0:T(8,128)S(1)}, u32[]{:S(2)}, u32[]{:S(2)}) async-start(f32[8,6,192]{2,1,0:T(8,128)} %bitcast.8), calls=%async_computation.1 | async-start | bytes 131072 | tf_op jit(solution)/shard_map/all_to_all | solution.py:30
  58.2 36.4 %reduce-scatter.2.cloned.1.call-start = ((), (), s32[]{:S(2)}) async-start(), calls=%async_computation.3 | async-start | bytes 655360 | tf_op jit(solution)/shard_map/reduce_scatter | solution.py:61
Sparse Core Ops, SparseCore 0:
  75.1 19.5 reduce-scatter.1
